TPU v7x, 32 devices: a whole 2x2x4 slice. The times are simulated.
32 devices in a mesh: rep: 8 (over z, x), tp: 4 (over y, core).
Axes of the slice: x: 2, y: 2, z: 4, core: 2. Of those that a mesh axis runs over, the one named last changes fastest.
Arguments:
- suffix_source: bfloat16 [8, 384, 4096], P('rep', None, 'tp'), may hold values from -6 to 6
- suffix_accept: bfloat16 [8, 384, 4096], P('rep', None, 'tp'), may hold values from -3 to 3
- suffix_address: bfloat16 [8, 384, 4096], P('rep', None, 'tp'), may hold values from -3 to 3
- guess_lane_source: bfloat16 [16, 16, 4096], P('rep', None, 'tp'), may hold values from -6 to 6
- guess_lane_accept: bfloat16 [16, 16, 4096], P('rep', None, 'tp'), may hold values from -3 to 3
- guess_lane_address: bfloat16 [16, 16, 4096], P('rep', None, 'tp'), may hold values from -3 to 3
- content_map: bfloat16 [4096, 4096], P(None, 'tp'), may hold values from -0.09375 to 0.09375
- forget_shrink_map: bfloat16 [4096, 128], replicated, may hold values from -0.09375 to 0.09375
- forget_expand_map: bfloat16 [128, 4096], P(None, 'tp'), may hold values from -0.35351562 to 0.35351562
- forget_lane_anchor: float32 [4096], P('tp'), may hold values from -12 to -3
- present_boost: float32 [4096], P('tp'), may hold values from -1.5 to 1.5
- content_blend_share: float32 [4096], P('tp'), may hold values from 0 to 1
- forget_blend_share: float32 [4096], P('tp'), may hold values from 0 to 1
- lane_normal_scale: float32 [4096], P('tp'), may hold values from 0.5 to 1.5
- lane_normal_shift: float32 [4096], P('tp'), may hold values from -1.2 to 1.2
- kernel_memory_saved: float32 [16, 64, 4096], P(None, 'rep', 'tp'), may hold values from -6 to 6
- prior_source_saved: bfloat16 [16, 64, 64], P(None, 'rep', 'tp'), may hold values from -6 to 6
- lane_owner: int32 [16], replicated, may hold values from 0 to 15, as said below
- request_spans: int32 [16], replicated, may hold values from 16 to 400, as said below
- admitted_guesses: int32 [16], replicated, may hold values from 0 to 16
Outputs:
- tail_out: bfloat16 [8, 384, 4096], P('rep', None, 'tp')
- draft_out: bfloat16 [16, 16, 4096], P('rep', None, 'tp')
- state_out: float32 [16, 64, 4096], P(None, 'rep', 'tp')
- shift_out: bfloat16 [16, 64, 64], P(None, 'rep', 'tp')
Inputs may be any that keep to these rules, and one draw needn't show every extreme that they name: `lane_owner`: a permutation of the request numbers. `request_spans`: exactly 1 request have 16 + 384 tokens and the others 16; a long request is always dealt to a slot s with s % 2 == 0; each aligned block of 8 consecutive groups holds exactly one group whose first slot is long; the tail buffers of groups whose first slot is not long are not read.
All inputs are finite; a program needn't handle non-finite values.
Results may differ from a plain program's by a relative error of at most 0.0051.
The roundings to bfloat16 on the way count: a program that leaves them out, or rounds other values in their place, can miss the bound.
Values may be sent and summed in bfloat16 or wider, within the bound.
No kernel may reach another device: no remote copies, remote signals or barrier semaphores. Data moves between devices by JAX's collectives and lax.ppermute only.
A program may use at most 128 MiB of HBM per device.

v0:
```python
import functools

import jax
import jax.numpy as jnp
from jax import lax
from jax.experimental import pallas as pl
from jax.experimental.pallas import tpu as pltpu
from jax.sharding import PartitionSpec as P

SPAN = 64
DRAFT = 16
QUAD = 4 * SPAN
PIECES = 3
LINE = 128
EXTRA = 16
TAIL_FIRST, TAIL_LAST, MIX_V, MIX_W = 0, 1, 2, 5
EPS = 0.00064
SAFE = -60.0
F32, BF16 = jnp.float32, jnp.bfloat16
VMEM_MIB = 62
SMEM = pl.BlockSpec(memory_space=pltpu.SMEM)
HBM = pl.BlockSpec(memory_space=pltpu.HBM)


def params(mib=VMEM_MIB):
    return pltpu.CompilerParams(vmem_limit_bytes=mib * 1024 * 1024)


def iota(shape, dim):
    return lax.broadcasted_iota(jnp.int32, shape, dim)


def split2(x, axis):
    high = x.astype(BF16)
    return jnp.concatenate([high, (x - high.astype(F32)).astype(BF16)], axis=axis)


def split3(x):
    high = x.astype(BF16)
    rest = x - high.astype(F32)
    mid = rest.astype(BF16)
    return high, mid, (rest - mid.astype(F32)).astype(BF16)


def dot(a, b):
    return jnp.dot(a, b, preferred_element_type=F32)


def dot_rows(a, b):
    return lax.dot_general(a, b, (((0,), (0,)), ((), ())), preferred_element_type=F32)


def dot_lanes(a, b):
    return lax.dot_general(a, b, (((1,), (1,)), ((), ())), preferred_element_type=F32)


def quad_lanes(p):
    if isinstance(p, int):
        return slice(p * QUAD, (p + 1) * QUAD)
    return pl.ds(pl.multiple_of(p * QUAD, QUAD), QUAD)


class Copies:
    def __init__(self, sems):
        self.sems, self.used = sems, 0

    def start(self, source, target):
        copy = pltpu.make_async_copy(source, target, self.sems.at[self.used])
        self.used += 1
        copy.start()
        return copy


def call(kernel, args, in_specs, outs, scratch, name, flops=0, moved=0, out_specs=None):
    return pl.pallas_call(
        kernel,
        in_specs=in_specs,
        out_specs=out_specs or [HBM] * len(outs),
        out_shape=[jax.ShapeDtypeStruct(s, t) for s, t in outs],
        scratch_shapes=scratch,
        compiler_params=params(),
        cost_estimate=pl.CostEstimate(flops=flops, bytes_accessed=moved, transcendentals=0),
        name=name,
    )(*args)


def pack_kernel(slots, owner, state, prior, out, held, cached, lines, sems):
    groups, rows, _ = out.shape
    width = state.shape[2]
    heads = prior.shape[2]
    go = Copies(sems)
    second = go.start(state, held)
    first = go.start(prior, cached)
    lines[...] = jnp.zeros_like(lines)
    first.wait()
    lines[:, :, 0:heads] = cached[...].astype(F32)
    second.wait()
    for g in range(groups):
        reqs = [owner[g * slots + s] for s in range(slots)]
        out[g, :, 0:width] = jnp.concatenate([held[q] for q in reqs], axis=0).astype(BF16)
        out[g, :, width:] = jnp.concatenate([lines[q] for q in reqs], axis=0).astype(BF16)


def pack(lane_owner, state, prior, groups):
    reqs, depth, width = state.shape
    slots = reqs // groups
    out = (groups, slots * depth, width + LINE)
    return pl.pallas_call(
        functools.partial(pack_kernel, slots),
        grid=(1,),
        in_specs=[SMEM, HBM, HBM],
        out_specs=pl.BlockSpec(out, lambda i: (0, 0, 0)),
        out_shape=jax.ShapeDtypeStruct(out, BF16),
        scratch_shapes=[
            pltpu.VMEM(state.shape, F32),
            pltpu.VMEM(prior.shape, BF16),
            pltpu.VMEM((reqs, depth, LINE), F32),
            pltpu.SemaphoreType.DMA((2,)),
        ],
        compiler_params=params(),
        name="pack",
    )(lane_owner, state, prior)


def small_kernel(slots, draft, tail, mix_v, mix_w, small, ends, shares, held, sems):
    copies = Copies(sems)
    last = tail.shape[0] - 16
    drafts = slots * DRAFT
    width = held.shape[1]
    waits = [
        copies.start(tail.at[pl.ds(0, 16), :], ends.at[0]),
        copies.start(tail.at[pl.ds(last, 16), :], ends.at[1]),
        copies.start(mix_v, shares.at[0]),
        copies.start(mix_w, shares.at[1]),
    ]
    waits += [copies.start(draft.at[s], held.at[pl.ds(s * DRAFT, DRAFT), :]) for s in range(slots)]
    row = iota((EXTRA, width), 0)
    for w in waits:
        w.wait()
    value = jnp.where(row == TAIL_FIRST, ends[0].astype(F32)[0:1], 0.0)
    value = jnp.where(row == TAIL_LAST, ends[1].astype(F32)[15:16], value)
    for n, base in enumerate((MIX_V, MIX_W)):
        for m, part in enumerate(split3(shares[n])):
            value = jnp.where(row == base + m, part.astype(F32), value)
    held[drafts:, :] = value.astype(BF16)
    copies.start(held, small).wait()


def small_payload(draft, tail, mix_v, mix_w):
    slots, _, width = draft.shape
    size = (slots * DRAFT + EXTRA, width)
    return call(
        functools.partial(small_kernel, slots),
        (draft, tail, mix_v, mix_w),
        [HBM] * 4,
        [(size, BF16)],
        [
            pltpu.VMEM((2, 16, width), BF16),
            pltpu.VMEM((2, 1, width), F32),
            pltpu.VMEM(size, BF16),
            pltpu.SemaphoreType.DMA((5 + slots,)),
        ],
        "small_payload",
    )[0]


def head_ones(scale=1.0):
    r, c = iota((QUAD, QUAD), 0), iota((QUAD, QUAD), 1)
    return jnp.where(r // SPAN == c // SPAN, scale, 0.0).astype(BF16)


def head_masks(dtype):
    lane = iota((1, QUAD), 1) // SPAN
    return [(lane == h).astype(F32).astype(dtype) for h in range(QUAD // SPAN)]


def by_head(x, masks):
    return jnp.concatenate([x * m for m in masks], axis=0)


def own_rows(x, depth):
    lane = iota((depth, QUAD), 1) // SPAN
    out = x[:depth]
    for h in range(1, QUAD // SPAN):
        out = jnp.where(lane == h, x[h * depth : (h + 1) * depth], out)
    return out


def down_state(line, ones):
    keep = iota((SPAN, QUAD), 0) == iota((SPAN, QUAD), 1) % SPAN
    both = dot(split2(jnp.where(keep, line, 0.0), 0), ones)
    return both[:SPAN] + both[SPAN:]


def gathered(keys, v):
    return own_rows(dot_rows(keys.astype(BF16), v), SPAN)


def sums_after(n):
    t, u = iota((n, 2 * n), 0), iota((n, 2 * n), 1) & (n - 1)
    return (u > t).astype(BF16)


def mixed(x, previous, share):
    return (x + (previous - x) * share).astype(BF16)


def shares_of(rest):
    take = lambda n: rest[n : n + 1] + rest[n + 1 : n + 2] + rest[n + 2 : n + 3]
    return take(MIX_V), take(MIX_W)


def draft_mixes(d, owns, is_long, slots):
    drafts = slots * DRAFT
    rest = d[drafts:]
    share_v, share_w = shares_of(rest)
    row = iota(d.shape, 0)
    previous = pltpu.roll(d, 1, 0)
    for s in range(slots):
        own = owns[s : s + 1]
        first = jnp.where(is_long[s], rest[TAIL_LAST : TAIL_LAST + 1], own)
        previous = jnp.where(row == s * DRAFT, first, previous)
        if s == 0:
            previous = jnp.where(row == drafts + TAIL_FIRST, own, previous)
    return mixed(d, previous, share_v), mixed(d, previous, share_w), share_v, share_w


def long_slots(owner, spans, slots):
    first = lax.axis_index("rep") * slots
    return [spans[owner[first + s]] > DRAFT for s in range(slots)]


def feature_block(j, width):
    return pl.ds(pl.multiple_of(jnp.bitwise_xor(lax.axis_index("tp"), j) * width, width), width)


def early_kernel(*refs):
    refs = list(refs)
    take = lambda n: [refs.pop(0) for _ in range(n)]
    xs_in, shares_in = take(2), take(4)
    shrink_in, weights = take(2)
    v_out, w_out, xs, shares, shrink, held, acc_v, acc_w, sems = take(9)
    width = xs.shape[2]
    go = Copies(sems)
    waits = []
    for j in range(2):
        block = feature_block(j, width)
        waits.append(
            [
                go.start(shares_in[2 * j], shares.at[2 * j]),
                go.start(shares_in[2 * j + 1], shares.at[2 * j + 1]),
                go.start(xs_in[j], xs.at[j]),
                go.start(shrink_in.at[block, :], shrink.at[j]),
                go.start(weights.at[block, :], held.at[j]),
            ]
        )
    for j in range(2):
        for w in waits[j]:
            w.wait()
        x = xs[j].astype(F32)
        previous = pltpu.roll(x, 1, 0)
        low = dot(mixed(x, previous, shares[2 * j + 1]), shrink[j])
        part = dot(mixed(x, previous, shares[2 * j]), held[j])
        if j == 0:
            acc_w[...] = low
            acc_v[...] = part
        else:
            acc_w[...] += low
            acc_v[...] += part
    outs = [go.start(acc_v, v_out), go.start(acc_w, w_out)]
    for w in outs:
        w.wait()


def early(xs, shares, shrink, weights):
    rows, width = xs[0].shape
    rank = shrink.shape[1]
    return call(
        early_kernel,
        (*xs, *shares, shrink, weights),
        [HBM] * 8,
        [((rows, width), F32), ((rows, rank), F32)],
        [
            pltpu.VMEM((2, rows, width), BF16),
            pltpu.VMEM((4, 1, width), F32),
            pltpu.VMEM((2, width, rank), BF16),
            pltpu.VMEM((2, width, width), BF16),
            pltpu.VMEM((rows, width), F32),
            pltpu.VMEM((rows, rank), F32),
            pltpu.SemaphoreType.DMA((12,)),
        ],
        "early",
        4 * rows * width * width,
        4 * width * width,
    )


def owns_kernel(slots, got_in, out, lines, held, sems):
    width = out.shape[1]
    copy = pltpu.make_async_copy(got_in.at[:, :, pl.ds(width, LINE)], lines, sems.at[0])
    copy.start()
    place = (iota((LINE, width), 0) == iota((LINE, width), 1) // SPAN).astype(BF16)
    keep = iota((SPAN, width), 0) == iota((SPAN, width), 1) % SPAN
    row = iota((EXTRA, width), 0)
    groups, per, _ = lines.shape
    depth = per // slots
    copy.wait()
    wide = lines[...].astype(F32)
    value = jnp.zeros((EXTRA, width), F32)
    for s in range(slots):
        mine = [wide[g, s * depth : (s + 1) * depth] for g in range(groups)]
        spread = dot(jnp.concatenate(mine, axis=0).astype(BF16), place)
        own = jnp.sum(jnp.where(keep, spread, 0.0), axis=0, keepdims=True)
        value = jnp.where(row == s, own, value)
    held[...] = value.astype(BF16)
    copy = pltpu.make_async_copy(held, out, sems.at[1])
    copy.start()
    copy.wait()


def own_inputs(got, slots, width):
    return call(
        functools.partial(owns_kernel, slots),
        (got,),
        [HBM],
        [((EXTRA, width), BF16)],
        [
            pltpu.VMEM((got.shape[0], got.shape[1], LINE), BF16),
            pltpu.VMEM((EXTRA, width), BF16),
            pltpu.SemaphoreType.DMA((2,)),
        ],
        "own_inputs",
    )[0]


def final_kernel(slots, copies, direct, *refs):
    refs = list(refs)
    take = lambda n: [refs.pop(0) for _ in range(n)]
    owner, spans, admitted = take(3)
    xs_in, smalls_in, owns_in, parts_in = take(2), take(copies), take(copies), take(2)
    shrink_in, expand_in, anchor_in, keys_in, draft_keys_in, got_in, weights = take(7)
    v_out, low_out, starts_out, back = take(4)
    xs, smalls, owns, part_v, part_w, shrink, expand, anchor, keys, draft_keys, got, held = take(12)
    v_held, w_held, low_held, starts, sems = take(5)

    tail, width = xs.shape[1:]
    rows = tail // PIECES
    quads = width // QUAD
    drafts = slots * DRAFT
    groups = got.shape[0]
    lines = SPAN // groups
    special = tail + drafts
    go = Copies(sems)
    blocks = [feature_block(j, width) for j in range(copies)]
    wait_small = [go.start(smalls_in[j], smalls.at[j]) for j in range(copies)]
    wait_small += [go.start(owns_in[j], owns.at[j]) for j in range(copies)]
    wait_x, wait_w = [], {}
    for n in range(2):
        wait_x.append(go.start(xs_in[n], xs.at[n]))
        if n == 0:
            wait_shrink = go.start(shrink_in, shrink)
        wait_w[2 + n] = go.start(weights.at[blocks[2 + n], :], held.at[2 + n])
    for j in range(2):
        wait_w[j] = go.start(weights.at[blocks[j], :], held.at[j])
    wait_part = [go.start(parts_in[0], part_v), go.start(parts_in[1], part_w)]
    wait_part += [go.start(expand_in, expand), go.start(anchor_in, anchor)]
    wait_keys = [go.start(keys_in, keys), go.start(draft_keys_in, draft_keys), go.start(got_in, got)]
    is_long = long_slots(owner, spans, slots)
    first_slot = lax.axis_index("rep") * slots
    counts = [admitted[owner[first_slot + s]] for s in range(slots)]

    for w in wait_small:
        w.wait()

    def drafts_of(j):
        return draft_mixes(smalls[j].astype(F32), owns[j].astype(F32), is_long, slots)

    acc_v = acc_w = None
    for n in range(2):
        dv, dw, share_v, share_w = drafts_of(2 + n)
        wait_x[n].wait()
        now = xs[n].astype(F32)
        previous = pltpu.roll(now, 1, 0)
        xv = jnp.concatenate([mixed(now, previous, share_v), dv], axis=0)
        xw = jnp.concatenate([mixed(now, previous, share_w), dw], axis=0)
        if n == 0:
            wait_shrink.wait()
        low = dot(xw, shrink[blocks[2 + n], :])
        wait_w[2 + n].wait()
        part = dot(xv, held[2 + n])
        acc_w = low if n == 0 else acc_w + low
        acc_v = part if n == 0 else acc_v + part
    draft_v, draft_w = acc_v[tail:], acc_w[tail:]
    for j in range(2):
        dv, dw, _, _ = drafts_of(j)
        draft_w = draft_w + dot(dw, shrink[blocks[j], :])
        wait_w[j].wait()
        draft_v = draft_v + dot(dv, held[j])
    for w in wait_part:
        w.wait()
    v_held[0:tail, :] = (acc_v[:tail] + part_v[...]).astype(BF16)
    v_held[tail:, :] = draft_v.astype(BF16)
    acc_w = jnp.concatenate([acc_w[:tail] + part_w[...], draft_w], axis=0)
    low_held[...] = jnp.tanh(acc_w).astype(BF16)
    rate = -jnp.exp(anchor[...] + dot(low_held[...], expand[...]))
    w_held[0:8, :] = jnp.where(iota((8, width), 0) == 0, 0.0, rate[:8])
    w_held[8:, :] = rate[8:]
    outs = [go.start(v_held, v_out), go.start(low_held, low_out)]
    for w in wait_keys:
        w.wait()

    ones = head_ones()
    after = sums_after(rows)
    t, u = iota((drafts, 2 * drafts), 0), iota((drafts, 2 * drafts), 1) & (drafts - 1)
    limit = jnp.zeros(t.shape, jnp.int32)
    row, row_limit = iota((drafts, QUAD), 0), jnp.zeros((drafts, QUAD), jnp.int32)
    for s in range(slots):
        limit = jnp.where((t >= s * DRAFT) & (t < (s + 1) * DRAFT), s * DRAFT + counts[s], limit)
        row_limit = jnp.where(
            (row >= s * DRAFT) & (row < (s + 1) * DRAFT), s * DRAFT + counts[s], row_limit
        )
    draft_after = ((u > t) & (u < limit)).astype(BF16)
    taken = row < row_limit
    for p in range(quads):
        lanes = quad_lanes(p)
        parts, rest = [], jnp.zeros((1, QUAD), F32)
        for n in reversed(range(PIECES)):
            w = w_held[n * rows : (n + 1) * rows, lanes]
            k = keys[n * rows : (n + 1) * rows, lanes].astype(F32)
            k = k * jnp.exp(dot(after, split2(w, 0)) + rest)
            if n == 0:
                k = jnp.where(iota(k.shape, 0) == 0, 0.0, k)
            parts.append(k)
            rest = rest + jnp.sum(w, axis=0, keepdims=True)
        gained = gathered(jnp.concatenate(parts[::-1], axis=0), v_held[0:tail, lanes])
        begin = [
            jnp.concatenate(
                [got[g, :, lanes].astype(F32)[s * lines : (s + 1) * lines] for g in range(groups)], axis=0
            )
            for s in range(slots)
        ]
        starts[0, :, lanes] = begin[0].astype(BF16)
        lift = jnp.exp(down_state(w_held[special : special + 1, lanes], ones))
        key = down_state(keys[0:16, lanes].astype(F32)[0:1], ones)
        state = lift * begin[0] + key * v_held[special : special + 16, lanes].astype(F32)[0:1]
        starts[1, :, lanes] = state.astype(BF16)
        state = jnp.exp(down_state(rest, ones)) * state + gained
        begin[0] = jnp.where(is_long[0], state, begin[0])
        w = w_held[tail:special, lanes]
        k = draft_keys[:, lanes].astype(F32) * jnp.exp(dot(draft_after, split2(w, 0)))
        k = jnp.where(taken, k, 0.0)
        v = v_held[tail:special, lanes]
        closed = []
        for s in range(slots):
            starts[2 + s, :, lanes] = begin[s].astype(BF16)
            mine = slice(s * DRAFT, (s + 1) * DRAFT)
            upto = jnp.sum(jnp.where(taken[mine], w[mine], 0.0), axis=0, keepdims=True)
            closed.append(jnp.exp(down_state(upto, ones)) * begin[s] + gathered(k[mine], v[mine]))
        if direct:
            for g in range(groups):
                part = jnp.concatenate([c[g * lines : (g + 1) * lines] for c in closed], axis=0)
                back[g, :, lanes] = part.astype(BF16)
        else:
            for s in range(slots):
                back[s, :, lanes] = closed[s].astype(BF16)
    outs.append(go.start(starts, starts_out))

    tokens = smalls[0].astype(F32)
    row = iota(tokens.shape, 0)
    place = (iota((LINE, width), 0) == iota((LINE, width), 1) // SPAN).astype(BF16)
    keep = iota((SPAN, width), 0) == iota((SPAN, width), 1) % SPAN
    edges = []
    for s in range(slots):
        own = owns[0].astype(F32)[s : s + 1]
        first = jnp.where(is_long[s], tokens[drafts + TAIL_LAST : drafts + TAIL_LAST + 1], own)
        chosen = jnp.sum(
            jnp.where(row == s * DRAFT + counts[s] - 1, tokens, 0.0), axis=0, keepdims=True
        )
        edge = jnp.where(counts[s] > 0, chosen, first)
        edges.append(dot_lanes(jnp.where(keep, edge, 0.0).astype(BF16), place))
    if direct:
        for g in range(groups):
            part = jnp.concatenate([e[g * lines : (g + 1) * lines] for e in edges], axis=0)
            back[g, :, width:] = part.astype(BF16)
    else:
        for s in range(slots):
            back[s, :, width:] = edges[s].astype(BF16)
    for w in outs:
        w.wait()


def final(scalars, xs, smalls, owns, parts, maps, keys, draft_keys, got, weights, slots):
    tail, width = xs[0].shape
    total = tail + smalls[0].shape[0]
    copies = len(smalls)
    groups = got.shape[0]
    rank = maps[0].shape[1]
    direct = SPAN // groups == 8
    back = (groups, got.shape[1]) if direct else (slots, SPAN)
    back = (*back, width + LINE)
    starts = (2 + slots, SPAN, width)
    args = [*scalars, *xs, *smalls, *owns, *parts, *maps, keys, draft_keys, got, weights]
    v, low, begins, ret = call(
        functools.partial(final_kernel, slots, copies, direct),
        args,
        [SMEM] * len(scalars) + [HBM] * (len(args) - len(scalars)),
        [((total, width), BF16), ((total, rank), BF16), (starts, BF16), (back, BF16)],
        [
            pltpu.VMEM((2, tail, width), BF16),
            pltpu.VMEM((copies, *smalls[0].shape), BF16),
            pltpu.VMEM((copies, *owns[0].shape), BF16),
            pltpu.VMEM((tail, width), F32),
            pltpu.VMEM((tail, rank), F32),
            pltpu.VMEM(maps[0].shape, BF16),
            pltpu.VMEM(maps[1].shape, BF16),
            pltpu.VMEM((1, width), F32),
            pltpu.VMEM(keys.shape, BF16),
            pltpu.VMEM(draft_keys.shape, BF16),
            pltpu.VMEM(got.shape, BF16),
            pltpu.VMEM((copies, width, width), BF16),
            pltpu.VMEM((total, width), BF16),
            pltpu.VMEM((total, width), F32),
            pltpu.VMEM((total, rank), BF16),
            pltpu.VMEM(starts, BF16),
            pltpu.SemaphoreType.DMA((32,)),
        ],
        "final",
        4 * tail * width * width,
        4 * width * width,
        [HBM, HBM, HBM, pl.BlockSpec(memory_space=pltpu.VMEM)],
    )
    if not direct:
        ret = ret.reshape(slots, groups, SPAN // groups, width + LINE).transpose(1, 0, 2, 3)
        ret = ret.reshape(groups, slots * SPAN // groups, width + LINE)
    return v, low, begins, ret


def levels_scores(r, k, rate, length, masks):
    n = r.shape[0]
    heads = len(masks)
    pieces = jnp.concatenate(split3(rate), axis=0)

    def level(n_level, total):
        half = lax.shift_left(jnp.int32(1), n_level)
        shift = n_level + 1
        t, u = iota((n, 3 * n), 0), iota((n, 3 * n), 1) % n
        edge = lax.shift_left(lax.shift_right_logical(t, shift), shift) + half
        after = (t >= edge) & (u >= edge) & (u < t)
        ahead = (t < edge) & (u > t) & (u < edge)
        decay = jnp.exp(dot((after | ahead).astype(BF16), pieces))
        row = iota(r.shape, 0)
        row_edge = lax.shift_left(lax.shift_right_logical(row, shift), shift) + half
        rt = jnp.where(row >= row_edge, r * decay, 0.0).astype(BF16)
        kt = jnp.where(row < row_edge, k * decay, 0.0)
        sc = dot_lanes(rt, by_head(kt, masks).astype(BF16))
        t2, s2 = iota((n, heads * n), 0), iota((n, heads * n), 1) & (n - 1)
        same = lax.shift_right_logical(t2, shift) == lax.shift_right_logical(s2, shift)
        return total + jnp.where(same, sc, 0.0)

    start = jnp.zeros((n, heads * n), F32)
    return lax.fori_loop(0, length.bit_length() - 1, level, start)


def answers(r, k, v, rate, boost, states, length, scaled, ones, masks):
    n = r[0].shape[0]
    count = n // length
    heads = len(masks)
    every = range(len(r))
    t, u = iota((n, 2 * n), 0), iota((n, 2 * n), 1) & (n - 1)
    t2, s2 = iota((n, heads * n), 0), iota((n, heads * n), 1) & (n - 1)
    earlier, keep = u < t, s2 < t2
    if count > 1:
        earlier = earlier & (u // length == t // length)
        keep = keep & (s2 // length == t2 // length)
    earlier = earlier.astype(BF16)
    before = [dot(earlier, split2(x, 0)) for x in rate]
    if scaled:
        middle = []
        for x in before:
            rows = [x[s * length + length // 2 :][:1] for s in range(count)]
            if count > 1:
                rows = [jnp.concatenate([jnp.broadcast_to(m, (length, QUAD)) for m in rows], axis=0)]
            middle.append(rows[0])
        rt = [(r[i] * jnp.exp(before[i] - middle[i])).astype(BF16) for i in every]
        kt = [(k[i] * jnp.exp(middle[i] - before[i] - rate[i])).astype(BF16) for i in every]
        sc = [dot_lanes(rt[i], by_head(kt[i], masks)) for i in every]
        sc = [jnp.where(keep, x, 0.0).astype(BF16) for x in sc]
    else:
        sc = [levels_scores(r[i], k[i], rate[i], length, masks).astype(BF16) for i in every]
    bonus = [dot((r[i] * k[i] * boost[i]).astype(BF16), ones) * v[i].astype(F32) for i in every]
    rs = [(r[i] * jnp.exp(before[i])).astype(BF16) for i in every]
    y = [dot(sc[i], by_head(v[i], masks)) + bonus[i] for i in every]
    for i in every:
        outer = [
            dot(rs[i][s * length : (s + 1) * length], by_head(states[i][s], masks))
            for s in range(count)
        ]
        y[i] = y[i] + (outer[0] if count == 1 else jnp.concatenate(outer, axis=0))
    return y


def normed(y, gain, bias, mean_ones):
    every = range(len(y))
    center = [x - dot(x.astype(BF16), mean_ones) for x in y]
    spread = [dot((x * x).astype(BF16), mean_ones) for x in center]
    return [
        (center[i] * lax.rsqrt(spread[i] + EPS) * gain[i] + bias[i]).astype(BF16) for i in every
    ]


def outputs_kernel(slots, *refs):
    refs = list(refs)
    take = lambda n: [refs.pop(0) for _ in range(n)]
    owner, spans = take(2)
    v_in, low_in, expand_in, anchor_in, r_in, k_in, rd_in, kd_in, starts_in = take(9)
    lines_in = take(3)
    tail_out, draft_out = take(2)
    low, expand, anchor, v_held, w_held, r_held, k_held, rd, kd, starts, lines, states, out_held, draft_held, sems, done = take(16)
    tail, width = out_held.shape
    rows = tail // PIECES
    quads = width // QUAD
    drafts = slots * DRAFT
    special = tail + drafts
    go = Copies(sems)
    is_long = spans[owner[lax.axis_index("rep") * slots]] > DRAFT

    def leaving(n):
        at = pl.ds(n * rows, rows)
        return pltpu.make_async_copy(out_held.at[at, :], tail_out.at[at, :], done.at[n])

    def send(n):
        leaving(n).start()

    late = pl.ds(tail, drafts + EXTRA)
    wait_rate = [go.start(low_in, low), go.start(expand_in, expand), go.start(anchor_in, anchor)]
    waits = [go.start(v_in.at[late, :], v_held.at[late, :])]
    waits += [go.start(rd_in, rd), go.start(kd_in, kd), go.start(starts_in, starts)]
    waits += [go.start(x, lines.at[n]) for n, x in enumerate(lines_in)]
    pieces = [pl.ds(n * rows, rows) for n in range(PIECES)]
    loads = []
    for at in pieces:
        loads.append(
            [
                go.start(r_in.at[at, :], r_held.at[at, :]),
                go.start(k_in.at[at, :], k_held.at[at, :]),
                go.start(v_in.at[at, :], v_held.at[at, :]),
            ]
        )
    ones, mean_ones = head_ones(), head_ones(1.0 / SPAN)
    masks = head_masks(BF16)
    for w in wait_rate:
        w.wait()
    rate = -jnp.exp(anchor[...] + dot(low[...], expand[...]))
    w_held[0:8, :] = jnp.where(iota((8, width), 0) == 0, 0.0, rate[:8])
    w_held[8:, :] = rate[8:]
    for w in waits:
        w.wait()

    def line(n, lanes):
        return lines[n, :, lanes]

    def draft_quads(which, scaled):
        lanes = [quad_lanes(p) for p in which]
        y = answers(
            [rd[:, at].astype(F32) for at in lanes],
            [kd[:, at].astype(F32) for at in lanes],
            [v_held[tail:special, at] for at in lanes],
            [w_held[tail:special, at] for at in lanes],
            [line(0, at) for at in lanes],
            [[starts[2 + s, :, at] for s in range(slots)] for at in lanes],
            DRAFT, scaled, ones, masks,
        )
        out = normed(y, [line(1, at) for at in lanes], [line(2, at) for at in lanes], mean_ones)
        for at, x in zip(lanes, out):
            draft_held[:, at] = x

    sums = [
        jnp.sum(w_held[tail + s * DRAFT : tail + (s + 1) * DRAFT, :], axis=0, keepdims=True)
        for s in range(slots)
    ]
    safe = jnp.min(jnp.concatenate(sums, axis=0)) > SAFE

    @pl.when(safe)
    def _():
        draft_quads(range(quads), True)

    @pl.when(jnp.logical_not(safe))
    def _():
        def body(p, carry):
            draft_quads([p], False)
            return carry

        lax.fori_loop(0, quads, body, 0)

    out_waits = [go.start(draft_held, draft_out)]

    def tail_quads(n, which, scaled, carry_on):
        lanes = [quad_lanes(p) for p in which]
        every = range(len(lanes))
        at = pieces[n] if isinstance(n, int) else pl.ds(pl.multiple_of(n * rows, rows), rows)
        r = [r_held[at, x].astype(F32) for x in lanes]
        k = [k_held[at, x].astype(F32) for x in lanes]
        v = [v_held[at, x] for x in lanes]
        rate = [w_held[at, x] for x in lanes]
        state = [states[:, x] for x in lanes]
        boost = [line(0, x) for x in lanes]
        zr, zk = r, k
        if not isinstance(n, int) or n == 0:
            first = (iota((rows, QUAD), 0) == 0) & (n == 0)
            zr, zk = [jnp.where(first, 0.0, x) for x in r], [jnp.where(first, 0.0, x) for x in k]
        y = answers(
            zr, zk, v, rate, boost, [[x.astype(BF16)] for x in state], rows, scaled, ones, masks
        )
        if not isinstance(n, int) or n == 0:
            for i in every:
                r0, k0 = r[i][0:8], k[i][0:8]
                v0 = v_held[special : special + EXTRA, lanes[i]].astype(F32)[0:1]
                y0 = dot(r0.astype(BF16), by_head(starts[0, :, lanes[i]], masks))
                y0 = y0 + dot((r0 * k0 * boost[i]).astype(BF16), ones) * v0
                y[i] = jnp.where(first, y0[0:1], y[i])
        out = normed(y, [line(1, x) for x in lanes], [line(2, x) for x in lanes], mean_ones)
        for i in every:
            out_held[at, lanes[i]] = out[i]
        if carry_on:
            after = sums_after(rows)
            kept = [down_state(jnp.sum(x, axis=0, keepdims=True), ones) for x in rate]
            late = [dot(after, split2(x, 0)) for x in rate]
            gain = [gathered(zk[i] * jnp.exp(late[i]), v[i]) for i in every]
            for i in every:
                states[:, lanes[i]] = jnp.exp(kept[i]) * state[i] + gain[i]

    @pl.when(is_long)
    def _():
        states[...] = starts[1].astype(F32)
        lowest = functools.reduce(
            jnp.minimum,
            [
                jnp.sum(w_held[n * rows : (n + 1) * rows, :], axis=0, keepdims=True)
                for n in range(PIECES)
            ],
        )
        fine = jnp.min(lowest) > SAFE

        @pl.when(fine)
        def _():
            for n in range(PIECES):
                for w in loads[n]:
                    w.wait()
                tail_quads(n, range(quads), True, n < PIECES - 1)
                send(n)

        @pl.when(jnp.logical_not(fine))
        def _():
            for group in loads:
                for w in group:
                    w.wait()

            def body(m, carry):
                tail_quads(m // quads, [m % quads], False, True)
                return carry

            lax.fori_loop(0, PIECES * quads, body, 0)
            for n in range(PIECES):
                send(n)

    @pl.when(jnp.logical_not(is_long))
    def _():
        for group in loads:
            for w in group:
                w.wait()
        out_held[...] = jnp.zeros_like(out_held)
        for n in range(PIECES):
            send(n)

    for w in out_waits:
        w.wait()
    for n in range(PIECES):
        leaving(n).wait()


def outputs(scalars, arrays, slots):
    v, low, expand, anchor, r, k, rd, kd, starts = arrays[:9]
    tail, width = r.shape
    drafts = slots * DRAFT
    args = [*scalars, *arrays]
    return call(
        functools.partial(outputs_kernel, slots),
        args,
        [SMEM] * len(scalars) + [HBM] * (len(args) - len(scalars)),
        [((tail, width), BF16), ((drafts, width), BF16)],
        [
            pltpu.VMEM(low.shape, BF16),
            pltpu.VMEM(expand.shape, BF16),
            pltpu.VMEM(anchor.shape, F32),
            pltpu.VMEM(v.shape, BF16),
            pltpu.VMEM(v.shape, F32),
            pltpu.VMEM(r.shape, BF16),
            pltpu.VMEM(k.shape, BF16),
            pltpu.VMEM(rd.shape, BF16),
            pltpu.VMEM(kd.shape, BF16),
            pltpu.VMEM(starts.shape, BF16),
            pltpu.VMEM((3, 1, width), F32),
            pltpu.VMEM((SPAN, width), F32),
            pltpu.VMEM((tail, width), BF16),
            pltpu.VMEM((drafts, width), BF16),
            pltpu.SemaphoreType.DMA((32,)),
            pltpu.SemaphoreType.DMA((PIECES,)),
        ],
        "outputs",
        16 * tail * width * LINE,
        16 * tail * width,
    )


def unpack_kernel(slots, owner, back, state_out, shift_out):
    reqs, lines, width = state_out.shape
    heads = shift_out.shape[2]
    for g in range(reqs // slots):
        rows = back[g].astype(F32)
        for s in range(slots):
            q = owner[g * slots + s]
            mine = rows[s * lines : (s + 1) * lines]
            state_out[q] = mine[:, :width]
            shift_out[q] = mine[:, width : width + heads].astype(BF16)


def unpack(lane_owner, back, slots, lines, width, heads):
    reqs = back.shape[0] * slots
    outs = [((reqs, lines, width), F32), ((reqs, lines, heads), BF16)]
    vmem = pl.BlockSpec(memory_space=pltpu.VMEM)
    return pl.pallas_call(
        functools.partial(unpack_kernel, slots),
        in_specs=[SMEM, vmem],
        out_specs=[vmem, vmem],
        out_shape=[jax.ShapeDtypeStruct(s, t) for s, t in outs],
        compiler_params=params(16),
        name="unpack",
    )(lane_owner, back)


def local(
    groups,
    copies,
    suffix_source,
    suffix_accept,
    suffix_address,
    guess_lane_source,
    guess_lane_accept,
    guess_lane_address,
    content_map,
    forget_shrink_map,
    forget_expand_map,
    forget_lane_anchor,
    present_boost,
    content_blend_share,
    forget_blend_share,
    lane_normal_scale,
    lane_normal_shift,
    kernel_memory_saved,
    prior_source_saved,
    lane_owner,
    request_spans,
    admitted_guesses,
):
    width = content_map.shape[1]
    slots = guess_lane_source.shape[0]
    drafts = slots * DRAFT
    lines = kernel_memory_saved.shape[1]
    line = lambda x: x.reshape(1, width)

    def flip(x, k):
        return lax.ppermute(x, "tp", [(i, i ^ k) for i in range(copies)])

    tail = suffix_source[0]
    keys = suffix_address[0]
    draft_keys = guess_lane_address.reshape(drafts, width)
    mixes = [line(content_blend_share), line(forget_blend_share)]
    cross, near = flip(tail, 2), flip(tail, 1)
    near_mixes = [flip(x, 1) for x in mixes]
    sent = pack(lane_owner, kernel_memory_saved, prior_source_saved, groups)
    got = lax.all_to_all(sent, "rep", 0, 0)
    part_v, part_w = early([tail, near], [*mixes, *near_mixes], forget_shrink_map, content_map)
    got, part_v, part_w = lax.optimization_barrier((got, part_v, part_w))
    owns = own_inputs(got, slots, width)
    small = small_payload(guess_lane_source, tail, *mixes)
    small_cross, small_near = flip(small, 2), flip(small, 1)
    cross, small_cross, owns = lax.optimization_barrier((cross, small_cross, owns))
    owns = [owns] + [flip(owns, k) for k in range(1, copies)]
    far = flip(cross, 1)
    smalls = [small, small_near, small_cross, flip(small_cross, 1)]
    anchor = line(forget_lane_anchor)
    v, low, starts, ret = final(
        (lane_owner, request_spans, admitted_guesses),
        [cross, far],
        smalls,
        owns,
        [part_v, part_w],
        (forget_shrink_map, forget_expand_map, anchor),
        keys,
        draft_keys,
        got,
        content_map,
        slots,
    )
    back = lax.all_to_all(ret, "rep", 0, 0)
    tail_out, draft_out = outputs(
        (lane_owner, request_spans),
        [
            v,
            low,
            forget_expand_map,
            anchor,
            suffix_accept[0],
            keys,
            guess_lane_accept.reshape(drafts, width),
            draft_keys,
            starts,
            line(present_boost),
            line(lane_normal_scale),
            line(lane_normal_shift),
        ],
        slots,
    )
    state_out, shift_out = unpack(lane_owner, back, slots, lines, width, width // SPAN)
    return (
        tail_out[None],
        draft_out.reshape(slots, DRAFT, width),
        state_out,
        shift_out,
    )


def solution(mesh):
    wide = P("rep", None, "tp")
    cached = P(None, "rep", "tp")
    placed = (wide,) * 6 + (P(None, "tp"), P(), P(None, "tp")) + (P("tp"),) * 6
    placed += (cached, cached, P(), P(), P())
    return jax.shard_map(
        functools.partial(local, mesh.shape["rep"], mesh.shape["tp"]),
        mesh=mesh,
        in_specs=placed,
        out_specs=(wide, wide, cached, cached),
        check_vma=False,
    )
```

profile of v0, /device:TPU:0, one launch (start us, length us, event | category | flops | bytes accessed | tf_op | source)
XLA Modules:
  0.0 60.1 jit_solution(351953500638329335)
XLA Ops:
  0.6 0.5 collective-permute-start.2
  1.1 2.6 %collective-permute-start = (bf16[384,1024]{1,0:T(8,128)(2,1)}, bf16[384,1024]{1,0:T(8,128)(2,1)S(1)}, u32[]{:S(2)}, u32[]{:S(2)}) collective-permute-start(bf16[384,1024]{1,0:T(8,128)(2,1)} %bitcast.16), channel_id=1, source_target_pairs={{0,2},{1,3},{2,0},{3,1},{4,6},{5,7},{6,4},{7,5},{8,10},{9,11},{10,... | collective-permute-start | bytes 2359304 | tf_op jit(solution)/shard_map/ppermute | solution.py:872
  3.7 2.5 %pack.1 = bf16[8,16,1152]{2,1,0:T(8,128)(2,1)} custom-call(s32[16]{0:T(128)} %owner.3, f32[16,8,1024]{2,1,0:T(8,128)} %state.1, bf16[16,8,16]{2,1,0:T(8,128)(2,1)} %prior.1), custom_call_target="tpu_custom_call" | custom-call | tf_op jit(solution)/shard_map/pack/pallas_call | solution.py:108
  6.2 5.8 %all-to-all-start = ((bf16[8,16,1152]{2,1,0:T(8,128)(2,1)}), bf16[8,16,1152]{2,1,0:T(8,128)(2,1)S(1)}, u32[]{:S(2)}, u32[]{:S(2)}) async-start(bf16[8,16,1152]{2,1,0:T(8,128)(2,1)} %pack.1), calls=%async_computation | async-start | bytes 589824 | tf_op jit(solution)/shard_map/all_to_all | solution.py:881
  12.0 0.0 collective-permute-start.3
  12.0 0.5 collective-permute-start.4
  12.5 1.6 %small_payload.1.refs_5_ = bf16[48,1024]{1,0:T(8,128)(2,1)} custom-call(bf16[2,16,1024]{2,1,0:T(8,128)(2,1)} %draft.1, bf16[384,1024]{1,0:T(8,128)(2,1)} %bitcast.17, f32[1,1024]{1,0:T(1,128)} %bitcast.24, f32[1,1024]{1,0:T(1,128)} %bitcast.27), custom_call_target="tpu_custom_call" | custom-call | tf_op jit(solution)/shard_map/small_payload/pallas_call | solution.py:75
  14.2 0.0 copy-start.5
  14.2 0.6 collective-permute-start.1
  14.7 0.0 collective-permute-done.3.refs_4_
  14.7 0.0 copy-start.11
  14.7 0.0 collective-permute-done.4.refs_5_
  14.8 0.0 copy-start.12
  14.8 0.0 collective-permute-done.2.refs_1_
  14.8 0.6 copy-done.11
  15.3 0.0 copy-done.12
  15.3 0.0 copy-start.4
  15.3 0.9 %copy-done.4 = bf16[384,1024]{1,0:T(8,128)(2,1)} copy-done((bf16[384,1024]{1,0:T(8,128)(2,1)}, bf16[384,1024]{1,0:T(8,128)(2,1)S(1)}, u32[]{:S(2)}) %copy-start.4) | copy-done | bytes 786456
  16.2 6.1 %early.1 = (f32[384,1024]{1,0:T(8,128)}, f32[384,128]{1,0:T(8,128)}) custom-call(bf16[384,1024]{1,0:T(8,128)(2,1)} %bitcast.18, bf16[384,1024]{1,0:T(8,128)(2,1)} %copy-done.4, f32[1,1024]{1,0:T(1,128)} %bitcast.25, f32[1,1024]{1,0:T(1,128)} %bitcast.28, f32[1,1024]{1,0:T(1,128)} %copy-done.11, f32[1,1024]{1,0:T(1,128)} %copy-done.12, ...), custom_call_target="tpu_custom_call" | custom-call | flops 1610612736 | bytes 4194304 | tf_op jit(solution)/shard_map/early/pallas_call | solution.py:75
  22.4 0.0 all-to-all-done.got_in.refs_20_
  22.4 0.0 copy-start.1
  22.4 0.7 %copy-done.1 = bf16[8,16,1152]{2,1,0:T(8,128)(2,1)} copy-done((bf16[8,16,1152]{2,1,0:T(8,128)(2,1)}, bf16[8,16,1152]{2,1,0:T(8,128)(2,1)S(1)}, u32[]{:S(2)}) %copy-start.1) | copy-done | bytes 294936
  23.1 1.6 %own_inputs.1.refs_9_ = bf16[16,1024]{1,0:T(8,128)(2,1)} custom-call(bf16[8,16,1152]{2,1,0:T(8,128)(2,1)} %copy-done.1), custom_call_target="tpu_custom_call" | custom-call | tf_op jit(solution)/shard_map/own_inputs/pallas_call | solution.py:75
  24.7 0.0 collective-permute-done.1.refs_7_
  24.7 0.0 collective-permute-done.refs_3_
  24.7 0.0 copy-start.2
  24.7 0.1 collective-permute-start.5
  24.8 0.0 copy-done.5
  24.8 0.5 collective-permute-start.6
  25.3 0.1 collective-permute-start.7
  25.4 1.6 %collective-permute-start.10 = (bf16[16,1024]{1,0:T(8,128)(2,1)}, bf16[16,1024]{1,0:T(8,128)(2,1)S(1)}, u32[]{:S(2)}, u32[]{:S(2)}) collective-permute-start(bf16[16,1024]{1,0:T(8,128)(2,1)} %own_inputs.1.refs_9_), channel_id=1, source_target_pairs={{0,3},{1,2},{2,1},{3,0},{4,7},{5,6},{6,5},{7,4},{8,11},{9,10},{10,... | collective-permute-start | bytes 98312 | tf_op jit(solution)/shard_map/ppermute | solution.py:872
  27.0 0.5 collective-permute-start.9
  27.5 0.0 collective-permute-done.6.refs_6_
  27.5 0.0 copy-start.6
  27.5 0.0 collective-permute-start.8
  27.5 1.4 %collective-permute-done.10.refs_12_ = bf16[16,1024]{1,0:T(8,128)(2,1)S(1)} collective-permute-done((bf16[16,1024]{1,0:T(8,128)(2,1)}, bf16[16,1024]{1,0:T(8,128)(2,1)S(1)}, u32[]{:S(2)}, u32[]{:S(2)}) %collective-permute-start.10) | collective-permute-done | bytes 32800 | tf_op jit(solution)/shard_map/ppermute | solution.py:872
  29.0 0.0 copy-start.8
  29.0 2.1 %collective-permute-done.9.refs_11_ = bf16[16,1024]{1,0:T(8,128)(2,1)S(1)} collective-permute-done((bf16[16,1024]{1,0:T(8,128)(2,1)}, bf16[16,1024]{1,0:T(8,128)(2,1)S(1)}, u32[]{:S(2)}, u32[]{:S(2)}) %collective-permute-start.9) | collective-permute-done | bytes 32800 | tf_op jit(solution)/shard_map/ppermute | solution.py:872
  31.1 0.0 copy-start.9
  31.1 0.0 collective-permute-done.8.refs_10_
  31.1 0.0 copy-start.10
  31.1 0.0 collective-permute-done.7.refs_8_
  31.1 0.0 copy-start.7
  31.1 0.0 collective-permute-done.5.refs_4_
  31.1 0.0 copy-start.3
  31.1 0.0 copy-done.2
  31.2 0.0 copy-done.6
  31.2 0.0 copy-done.8
  31.2 0.5 copy-done.9
  31.7 0.0 copy-done.10
  31.7 0.0 copy-done.7
  31.8 0.3 copy-done.3
  32.0 0.0 copy-start
  32.0 11.9 %final.1 = (bf16[432,1024]{1,0:T(8,128)(2,1)}, bf16[432,128]{1,0:T(8,128)(2,1)}, bf16[4,64,1024]{2,1,0:T(8,128)(2,1)}, bf16[8,16,1152]{2,1,0:T(8,128)(2,1)}) custom-call(s32[16]{0:T(128)} %owner.3, s32[16]{0:T(128)} %refs_1_.3, s32[16]{0:T(128)} %refs_2_.1, bf16[384,1024]{1,0:T(8,128)(2,1)} %copy-done.2, bf16[384,1024]{1,0:T(8,128)(2,1)} %copy-done.3, ...), custom_call_target="tpu_custom_call" | custom-call | flops 1610612736 | bytes 4194304 | tf_op jit(solution)/shard_map/final/pallas_call | solution.py:75
  44.0 6.0 %all-to-all-start.1 = ((bf16[8,16,1152]{2,1,0:T(8,128)(2,1)}), bf16[8,16,1152]{2,1,0:T(8,128)(2,1)S(1)}, u32[]{:S(2)}, u32[]{:S(2)}) async-start(bf16[8,16,1152]{2,1,0:T(8,128)(2,1)} %get-tuple-element.33), calls=%async_computation.1 | async-start | bytes 589824 | tf_op jit(solution)/shard_map/all_to_all | solution.py:905
  50.0 4.5 %outputs.1 = (bf16[384,1024]{1,0:T(8,128)(2,1)}, bf16[32,1024]{1,0:T(8,128)(2,1)}) custom-call(s32[16]{0:T(128)} %owner.3, s32[16]{0:T(128)} %refs_1_.3, bf16[432,1024]{1,0:T(8,128)(2,1)} %get-tuple-element.28.refs_2_, bf16[432,128]{1,0:T(8,128)(2,1)} %get-tuple-element.29.refs_3_, bf16[128,1024]{1,0:T(8,128)(2,1)} %refs_4_.1, f32[1,1024]{1,0:T(1,128)} %bitcast.30, ...), custom_call_target="tpu_custom_call" | custom-call | flops 805306368 | bytes 6291456 | tf_op jit(solution)/shard_map/outputs/pallas_call | solution.py:75
  54.5 4.2 %all-to-all-done.1.back = bf16[8,16,1152]{2,1,0:T(8,128)(2,1)S(1)} async-done(((bf16[8,16,1152]{2,1,0:T(8,128)(2,1)}), bf16[8,16,1152]{2,1,0:T(8,128)(2,1)S(1)}, u32[]{:S(2)}, u32[]{:S(2)}) %all-to-all-start.1) | async-done | bytes 294944 | tf_op jit(solution)/shard_map/all_to_all | solution.py:905
  58.7 0.0 copy-done
  58.8 1.4 %unpack.1 = (f32[16,8,1024]{2,1,0:T(8,128)}, bf16[16,8,16]{2,1,0:T(8,128)(2,1)}) custom-call(s32[16]{0:T(128)S(1)} %copy-done, bf16[8,16,1152]{2,1,0:T(8,128)(2,1)S(1)} %all-to-all-done.1.back), custom_call_target="tpu_custom_call" | custom-call | tf_op jit(solution)/shard_map/unpack/pallas_call | solution.py:831
Async XLA Ops:
  0.6 14.1 %collective-permute-start.2 = (bf16[384,1024]{1,0:T(8,128)(2,1)}, bf16[384,1024]{1,0:T(8,128)(2,1)S(1)}, u32[]{:S(2)}, u32[]{:S(2)}) collective-permute-start(bf16[384,1024]{1,0:T(8,128)(2,1)} %bitcast.15), channel_id=1, source_target_pairs={{0,1},{1,0},{2,3},{3,2},{4,5},{5,4},{6,7},{7,6},{8,9},{9,8},{10,11... | collective-permute-start | bytes 2359304 | tf_op jit(solution)/shard_map/ppermute | solution.py:872
  1.1 23.6 %collective-permute-start = (bf16[384,1024]{1,0:T(8,128)(2,1)}, bf16[384,1024]{1,0:T(8,128)(2,1)S(1)}, u32[]{:S(2)}, u32[]{:S(2)}) collective-permute-start(bf16[384,1024]{1,0:T(8,128)(2,1)} %bitcast.16), channel_id=1, source_target_pairs={{0,2},{1,3},{2,0},{3,1},{4,6},{5,7},{6,4},{7,5},{8,10},{9,11},{10,... | collective-permute-start | bytes 2359304 | tf_op jit(solution)/shard_map/ppermute | solution.py:872
  6.2 16.2 %all-to-all-start = ((bf16[8,16,1152]{2,1,0:T(8,128)(2,1)}), bf16[8,16,1152]{2,1,0:T(8,128)(2,1)S(1)}, u32[]{:S(2)}, u32[]{:S(2)}) async-start(bf16[8,16,1152]{2,1,0:T(8,128)(2,1)} %pack.1), calls=%async_computation | async-start | bytes 589824 | tf_op jit(solution)/shard_map/all_to_all | solution.py:881
  12.0 2.7 %collective-permute-start.3 = (f32[1,1024]{1,0:T(1,128)}, f32[1,1024]{1,0:T(1,128)S(1)}, u32[]{:S(2)}, u32[]{:S(2)}) collective-permute-start(f32[1,1024]{1,0:T(1,128)} %bitcast.23), channel_id=1, source_target_pairs={{0,1},{1,0},{2,3},{3,2},{4,5},{5,4},{6,7},{7,6},{8,9},{9,8},{10,11... | collective-permute-start | bytes 12296 | tf_op jit(solution)/shard_map/ppermute | solution.py:872
  12.0 2.7 %collective-permute-start.4 = (f32[1,1024]{1,0:T(1,128)}, f32[1,1024]{1,0:T(1,128)S(1)}, u32[]{:S(2)}, u32[]{:S(2)}) collective-permute-start(f32[1,1024]{1,0:T(1,128)} %bitcast.26), channel_id=1, source_target_pairs={{0,1},{1,0},{2,3},{3,2},{4,5},{5,4},{6,7},{7,6},{8,9},{9,8},{10,11... | collective-permute-start | bytes 12296 | tf_op jit(solution)/shard_map/ppermute | solution.py:872
  14.2 10.7 %copy-start.5 = (bf16[48,1024]{1,0:T(8,128)(2,1)S(1)}, bf16[48,1024]{1,0:T(8,128)(2,1)}, u32[]{:S(2)}) copy-start(bf16[48,1024]{1,0:T(8,128)(2,1)} %small_payload.1.refs_5_) | copy-start | bytes 294916
  14.2 10.5 %collective-permute-start.1 = (bf16[48,1024]{1,0:T(8,128)(2,1)}, bf16[48,1024]{1,0:T(8,128)(2,1)}, u32[]{:S(2)}, u32[]{:S(2)}) collective-permute-start(bf16[48,1024]{1,0:T(8,128)(2,1)} %small_payload.1.refs_5_), channel_id=1, source_target_pairs={{0,2},{1,3},{2,0},{3,1},{4,6},{5,7},{6,4},{7,5},{8,10},{9,11},{10,... | collective-permute-start | bytes 294920 | tf_op jit(solution)/shard_map/ppermute | solution.py:872
  14.7 0.6 copy-start.11
  14.8 0.6 copy-start.12
  15.3 0.9 %copy-start.4 = (bf16[384,1024]{1,0:T(8,128)(2,1)}, bf16[384,1024]{1,0:T(8,128)(2,1)S(1)}, u32[]{:S(2)}) copy-start(bf16[384,1024]{1,0:T(8,128)(2,1)S(1)} %collective-permute-done.2.refs_1_) | copy-start | bytes 2359300
  22.4 0.7 %copy-start.1 = (bf16[8,16,1152]{2,1,0:T(8,128)(2,1)}, bf16[8,16,1152]{2,1,0:T(8,128)(2,1)S(1)}, u32[]{:S(2)}) copy-start(bf16[8,16,1152]{2,1,0:T(8,128)(2,1)S(1)} %all-to-all-done.got_in.refs_20_) | copy-start | bytes 884740
  24.7 6.4 %copy-start.2 = (bf16[384,1024]{1,0:T(8,128)(2,1)}, bf16[384,1024]{1,0:T(8,128)(2,1)S(1)}, u32[]{:S(2)}) copy-start(bf16[384,1024]{1,0:T(8,128)(2,1)S(1)} %collective-permute-done.refs_3_) | copy-start | bytes 2359300
  24.7 6.4 %collective-permute-start.5 = (bf16[384,1024]{1,0:T(8,128)(2,1)S(1)}, bf16[384,1024]{1,0:T(8,128)(2,1)S(1)}, u32[]{:S(2)}, u32[]{:S(2)}) collective-permute-start(bf16[384,1024]{1,0:T(8,128)(2,1)S(1)} %collective-permute-done.refs_3_), channel_id=1, source_target_pairs={{0,1},{1,0},{2,3},{3,2},{4,5},{5,4},{6,7},{7,6},{8,9},{9,8},{10,11... | collective-permute-start | bytes 2359304 | tf_op jit(solution)/shard_map/ppermute | solution.py:872
  24.8 2.6 %collective-permute-start.6 = (bf16[48,1024]{1,0:T(8,128)(2,1)S(1)}, bf16[48,1024]{1,0:T(8,128)(2,1)S(1)}, u32[]{:S(2)}, u32[]{:S(2)}) collective-permute-start(bf16[48,1024]{1,0:T(8,128)(2,1)S(1)} %copy-done.5), channel_id=1, source_target_pairs={{0,1},{1,0},{2,3},{3,2},{4,5},{5,4},{6,7},{7,6},{8,9},{9,8},{10,11... | collective-permute-start | bytes 294920 | tf_op jit(solution)/shard_map/ppermute | solution.py:872
  25.3 5.8 %collective-permute-start.7 = (bf16[48,1024]{1,0:T(8,128)(2,1)}, bf16[48,1024]{1,0:T(8,128)(2,1)S(1)}, u32[]{:S(2)}, u32[]{:S(2)}) collective-permute-start(bf16[48,1024]{1,0:T(8,128)(2,1)} %collective-permute-done.1.refs_7_), channel_id=1, source_target_pairs={{0,1},{1,0},{2,3},{3,2},{4,5},{5,4},{6,7},{7,6},{8,9},{9,8},{10,11... | collective-permute-start | bytes 294920 | tf_op jit(solution)/shard_map/ppermute | solution.py:872
  25.4 3.6 %collective-permute-start.10 = (bf16[16,1024]{1,0:T(8,128)(2,1)}, bf16[16,1024]{1,0:T(8,128)(2,1)S(1)}, u32[]{:S(2)}, u32[]{:S(2)}) collective-permute-start(bf16[16,1024]{1,0:T(8,128)(2,1)} %own_inputs.1.refs_9_), channel_id=1, source_target_pairs={{0,3},{1,2},{2,1},{3,0},{4,7},{5,6},{6,5},{7,4},{8,11},{9,10},{10,... | collective-permute-start | bytes 98312 | tf_op jit(solution)/shard_map/ppermute | solution.py:872
  27.0 4.1 %collective-permute-start.9 = (bf16[16,1024]{1,0:T(8,128)(2,1)}, bf16[16,1024]{1,0:T(8,128)(2,1)S(1)}, u32[]{:S(2)}, u32[]{:S(2)}) collective-permute-start(bf16[16,1024]{1,0:T(8,128)(2,1)} %own_inputs.1.refs_9_), channel_id=1, source_target_pairs={{0,2},{1,3},{2,0},{3,1},{4,6},{5,7},{6,4},{7,5},{8,10},{9,11},{10,... | collective-permute-start | bytes 98312 | tf_op jit(solution)/shard_map/ppermute | solution.py:872
  27.5 3.7 %copy-start.6 = (bf16[48,1024]{1,0:T(8,128)(2,1)}, bf16[48,1024]{1,0:T(8,128)(2,1)S(1)}, u32[]{:S(2)}) copy-start(bf16[48,1024]{1,0:T(8,128)(2,1)S(1)} %collective-permute-done.6.refs_6_) | copy-start | bytes 294916
  27.5 3.6 %collective-permute-start.8 = (bf16[16,1024]{1,0:T(8,128)(2,1)}, bf16[16,1024]{1,0:T(8,128)(2,1)S(1)}, u32[]{:S(2)}, u32[]{:S(2)}) collective-permute-start(bf16[16,1024]{1,0:T(8,128)(2,1)} %own_inputs.1.refs_9_), channel_id=1, source_target_pairs={{0,1},{1,0},{2,3},{3,2},{4,5},{5,4},{6,7},{7,6},{8,9},{9,8},{10,11... | collective-permute-start | bytes 98312 | tf_op jit(solution)/shard_map/ppermute | solution.py:872
  29.0 2.2 %copy-start.8 = (bf16[16,1024]{1,0:T(8,128)(2,1)}, bf16[16,1024]{1,0:T(8,128)(2,1)S(1)}, u32[]{:S(2)}) copy-start(bf16[16,1024]{1,0:T(8,128)(2,1)S(1)} %collective-permute-done.10.refs_12_) | copy-start | bytes 98308
  31.1 0.6 %copy-start.9 = (bf16[16,1024]{1,0:T(8,128)(2,1)}, bf16[16,1024]{1,0:T(8,128)(2,1)S(1)}, u32[]{:S(2)}) copy-start(bf16[16,1024]{1,0:T(8,128)(2,1)S(1)} %collective-permute-done.9.refs_11_) | copy-start | bytes 98308
  31.1 0.6 %copy-start.10 = (bf16[16,1024]{1,0:T(8,128)(2,1)}, bf16[16,1024]{1,0:T(8,128)(2,1)S(1)}, u32[]{:S(2)}) copy-start(bf16[16,1024]{1,0:T(8,128)(2,1)S(1)} %collective-permute-done.8.refs_10_) | copy-start | bytes 98308
  31.1 0.7 %copy-start.7 = (bf16[48,1024]{1,0:T(8,128)(2,1)}, bf16[48,1024]{1,0:T(8,128)(2,1)S(1)}, u32[]{:S(2)}) copy-start(bf16[48,1024]{1,0:T(8,128)(2,1)S(1)} %collective-permute-done.7.refs_8_) | copy-start | bytes 294916
  31.1 0.9 %copy-start.3 = (bf16[384,1024]{1,0:T(8,128)(2,1)}, bf16[384,1024]{1,0:T(8,128)(2,1)S(1)}, u32[]{:S(2)}) copy-start(bf16[384,1024]{1,0:T(8,128)(2,1)S(1)} %collective-permute-done.5.refs_4_) | copy-start | bytes 2359300
  32.0 26.7 %copy-start = (s32[16]{0:T(128)S(1)}, s32[16]{0:T(128)}, u32[]{:S(2)}) copy-start(s32[16]{0:T(128)} %owner.3) | copy-start | bytes 196
  44.0 14.8 %all-to-all-start.1 = ((bf16[8,16,1152]{2,1,0:T(8,128)(2,1)}), bf16[8,16,1152]{2,1,0:T(8,128)(2,1)S(1)}, u32[]{:S(2)}, u32[]{:S(2)}) async-start(bf16[8,16,1152]{2,1,0:T(8,128)(2,1)} %get-tuple-element.33), calls=%async_computation.1 | async-start | bytes 589824 | tf_op jit(solution)/shard_map/all_to_all | solution.py:905
where the time goes:
time: 60.6 us; the launch traced here: 60.1 us
  Pallas kernels  29.7 us (49%)
  starting transfers between devices  18.8 us (31%)
  waiting for transfers between devices  7.82 us (13%)
  local copies, waits for them, and re-layouts  3.05 us (5%)
  between operations  0.84 us (1%)
    pallas_call x5, Pallas kernels, call(): pl.pallas_call(kernel, in_specs=in_specs, out_specs=out_specs or [HBM] *...  25.8 us
    ppermute x11, starting transfers between devices, flip(): return lax.ppermute(x, 'tp', [(i, i ^ k) for i in range(copies)])  6.93 us
    all_to_all x1, starting transfers between devices, local(): back = lax.all_to_all(ret, 'rep', 0, 0)  6.01 us
    all_to_all x1, starting transfers between devices, local(): got = lax.all_to_all(sent, 'rep', 0, 0)  5.82 us
    all_to_all x1, waiting for transfers between devices, local(): back = lax.all_to_all(ret, 'rep', 0, 0)  4.21 us
    ppermute x11, waiting for transfers between devices, flip(): return lax.ppermute(x, 'tp', [(i, i ^ k) for i in range(copies)])  3.6 us
    unnamed x26, local copies, waits for them, and re-layouts  3.05 us
    pallas_call x1, Pallas kernels, pack(): pl.pallas_call(functools.partial(pack_kernel, slots), grid=(1,), in_specs...  2.47 us
  transfers between devices with their start and end apart: 13, of which 3 were waited for; matrix products, arithmetic and copies ran while one was open for 0% of the time, Pallas kernels for 27%

commit v1 on v0

--- a/solution.py
+++ b/solution.py
@@ -71,14 +71,14 @@
         return copy
 
 
-def call(kernel, args, in_specs, outs, scratch, name, flops=0, moved=0, out_specs=None):
+def call(kernel, args, in_specs, outs, scratch, name, flops=0, moved=0, out_specs=None, mib=VMEM_MIB):
     return pl.pallas_call(
         kernel,
         in_specs=in_specs,
         out_specs=out_specs or [HBM] * len(outs),
         out_shape=[jax.ShapeDtypeStruct(s, t) for s, t in outs],
         scratch_shapes=scratch,
-        compiler_params=params(),
+        compiler_params=params(mib),
         cost_estimate=pl.CostEstimate(flops=flops, bytes_accessed=moved, transcendentals=0),
         name=name,
     )(*args)
@@ -330,6 +330,7 @@
             pltpu.SemaphoreType.DMA((2,)),
         ],
         "own_inputs",
+        mib=8,
     )[0]
 
 

time: 60.6 us -> 59.9 us (0.988)
  waiting for transfers between devices: 7.82 us -> 9.4 us
  Pallas kernels: 29.7 us -> 28.4 us
  local copies, waits for them, and re-layouts: 3.05 us -> 2.36 us
    ppermute x11, waiting for transfers between devices: 3.6 us -> 5.19 us  [flip(): return lax.ppermute(x, 'tp', [(i, i ^ k) for i in range(copies)])]
    pallas_call x5, Pallas kernels: 25.8 us -> 24.5 us  [call(): pl.pallas_call(kernel, in_specs=in_specs, out_specs=out_specs or [HBM] *...]
    unnamed x26 -> x28, local copies, waits for them, and re-layouts: 3.05 us -> 2.36 us
  transfers between devices with their start and end apart: 13 -> 13, of which waited for: 3 -> 4; matrix products, arithmetic and copies ran while one was open for 0% -> 0% of each run, Pallas kernels for 27% -> 25%
where the time goes in v1:
time: 59.9 us; the launch traced here: 59.5 us
  Pallas kernels  28.4 us (47%)
  starting transfers between devices  18.5 us (31%)
  waiting for transfers between devices  9.4 us (16%)
  local copies, waits for them, and re-layouts  2.36 us (4%)
  between operations  0.81 us (1%)
    pallas_call x5, Pallas kernels, call(): pl.pallas_call(kernel, in_specs=in_specs, out_specs=out_specs or [HBM] *...  24.5 us
    ppermute x11, starting transfers between devices, flip(): return lax.ppermute(x, 'tp', [(i, i ^ k) for i in range(copies)])  6.87 us
    all_to_all x1, starting transfers between devices, local(): back = lax.all_to_all(ret, 'rep', 0, 0)  5.82 us
    all_to_all x1, starting transfers between devices, local(): got = lax.all_to_all(sent, 'rep', 0, 0)  5.82 us
    ppermute x11, waiting for transfers between devices, flip(): return lax.ppermute(x, 'tp', [(i, i ^ k) for i in range(copies)])  5.19 us
    all_to_all x1, waiting for transfers between devices, local(): back = lax.all_to_all(ret, 'rep', 0, 0)  4.21 us
    pallas_call x1, Pallas kernels, pack(): pl.pallas_call(functools.partial(pack_kernel, slots), grid=(1,), in_specs...  2.47 us
    unnamed x28, local copies, waits for them, and re-layouts  2.36 us
  transfers between devices with their start and end apart: 13, of which 4 were waited for; matrix products, arithmetic and copies ran while one was open for 0% of the time, Pallas kernels for 25%

profile of v1, /device:TPU:0, one launch (start us, length us, event | category | flops | bytes accessed | tf_op | source)
XLA Modules:
  0.0 59.5 jit_solution(4261881202888991212)
XLA Ops:
  0.6 0.5 collective-permute-start.2
  1.1 2.6 %collective-permute-start = (bf16[384,1024]{1,0:T(8,128)(2,1)}, bf16[384,1024]{1,0:T(8,128)(2,1)S(1)}, u32[]{:S(2)}, u32[]{:S(2)}) collective-permute-start(bf16[384,1024]{1,0:T(8,128)(2,1)} %bitcast.16), channel_id=1, source_target_pairs={{0,2},{1,3},{2,0},{3,1},{4,6},{5,7},{6,4},{7,5},{8,10},{9,11},{10,... | collective-permute-start | bytes 2359304 | tf_op jit(solution)/shard_map/ppermute | solution.py:873
  3.7 2.5 %pack.1 = bf16[8,16,1152]{2,1,0:T(8,128)(2,1)} custom-call(s32[16]{0:T(128)} %owner.3, f32[16,8,1024]{2,1,0:T(8,128)} %state.1, bf16[16,8,16]{2,1,0:T(8,128)(2,1)} %prior.1), custom_call_target="tpu_custom_call" | custom-call | tf_op jit(solution)/shard_map/pack/pallas_call | solution.py:108
  6.2 5.8 %all-to-all-start = ((bf16[8,16,1152]{2,1,0:T(8,128)(2,1)}), bf16[8,16,1152]{2,1,0:T(8,128)(2,1)S(1)}, u32[]{:S(2)}, u32[]{:S(2)}) async-start(bf16[8,16,1152]{2,1,0:T(8,128)(2,1)} %pack.1), calls=%async_computation | async-start | bytes 589824 | tf_op jit(solution)/shard_map/all_to_all | solution.py:882
  12.0 0.0 collective-permute-start.3
  12.0 0.5 collective-permute-start.4
  12.5 1.6 %small_payload.1.refs_5_ = bf16[48,1024]{1,0:T(8,128)(2,1)} custom-call(bf16[2,16,1024]{2,1,0:T(8,128)(2,1)} %draft.1, bf16[384,1024]{1,0:T(8,128)(2,1)} %bitcast.17, f32[1,1024]{1,0:T(1,128)} %bitcast.24, f32[1,1024]{1,0:T(1,128)} %bitcast.27), custom_call_target="tpu_custom_call" | custom-call | tf_op jit(solution)/shard_map/small_payload/pallas_call | solution.py:75
  14.1 0.0 copy-start.6
  14.2 0.6 collective-permute-start.1
  14.7 0.0 collective-permute-done.3.refs_4_
  14.7 0.0 copy-start.12
  14.7 0.0 collective-permute-done.4.refs_5_
  14.7 0.0 copy-start.13
  14.7 0.0 collective-permute-done.2.refs_1_
  14.8 0.6 copy-done.12
  15.3 0.0 copy-done.13
  15.3 0.0 copy-start.5
  15.3 0.9 %copy-done.5 = bf16[384,1024]{1,0:T(8,128)(2,1)} copy-done((bf16[384,1024]{1,0:T(8,128)(2,1)}, bf16[384,1024]{1,0:T(8,128)(2,1)S(1)}, u32[]{:S(2)}) %copy-start.5) | copy-done | bytes 786456
  16.2 6.2 %early.1 = (f32[384,1024]{1,0:T(8,128)}, f32[384,128]{1,0:T(8,128)}) custom-call(bf16[384,1024]{1,0:T(8,128)(2,1)} %bitcast.18, bf16[384,1024]{1,0:T(8,128)(2,1)} %copy-done.5, f32[1,1024]{1,0:T(1,128)} %bitcast.25, f32[1,1024]{1,0:T(1,128)} %bitcast.28, f32[1,1024]{1,0:T(1,128)} %copy-done.12, f32[1,1024]{1,0:T(1,128)} %copy-done.13, ...), custom_call_target="tpu_custom_call" | custom-call | flops 1610612736 | bytes 4194304 | tf_op jit(solution)/shard_map/early/pallas_call | solution.py:75
  22.4 0.0 all-to-all-done.got_in.refs_20_
  22.4 0.0 copy-start
  22.4 0.3 own_inputs.1.refs_9_
  22.7 0.0 copy-start.1
  22.7 1.6 %collective-permute-done.1.refs_7_ = bf16[48,1024]{1,0:T(8,128)(2,1)} collective-permute-done((bf16[48,1024]{1,0:T(8,128)(2,1)}, bf16[48,1024]{1,0:T(8,128)(2,1)}, u32[]{:S(2)}, u32[]{:S(2)}) %collective-permute-start.1) | collective-permute-done | bytes 98336 | tf_op jit(solution)/shard_map/ppermute | solution.py:873
  24.3 0.0 collective-permute-done.refs_3_
  24.3 0.0 copy-start.3
  24.3 0.0 collective-permute-start.5
  24.3 0.0 copy-done.6
  24.3 0.5 collective-permute-start.6
  24.8 0.1 collective-permute-start.7
  24.9 1.8 %collective-permute-start.10 = (bf16[16,1024]{1,0:T(8,128)(2,1)S(1)}, bf16[16,1024]{1,0:T(8,128)(2,1)S(1)}, u32[]{:S(2)}, u32[]{:S(2)}) collective-permute-start(bf16[16,1024]{1,0:T(8,128)(2,1)S(1)} %own_inputs.1.refs_9_), channel_id=1, source_target_pairs={{0,3},{1,2},{2,1},{3,0},{4,7},{5,6},{6,5},{7,4},{8,11},{9,10},{10,... | collective-permute-start | bytes 98312 | tf_op jit(solution)/shard_map/ppermute | solution.py:873
  26.7 0.3 collective-permute-start.9
  27.0 0.0 collective-permute-done.6.refs_6_
  27.0 0.0 copy-start.7
  27.0 0.0 collective-permute-start.8
  27.0 1.3 %collective-permute-done.10.refs_12_ = bf16[16,1024]{1,0:T(8,128)(2,1)S(1)} collective-permute-done((bf16[16,1024]{1,0:T(8,128)(2,1)S(1)}, bf16[16,1024]{1,0:T(8,128)(2,1)S(1)}, u32[]{:S(2)}, u32[]{:S(2)}) %collective-permute-start.10) | collective-permute-done | bytes 32800 | tf_op jit(solution)/shard_map/ppermute | solution.py:873
  28.3 0.0 copy-start.9
  28.3 2.3 %collective-permute-done.9.refs_11_ = bf16[16,1024]{1,0:T(8,128)(2,1)S(1)} collective-permute-done((bf16[16,1024]{1,0:T(8,128)(2,1)S(1)}, bf16[16,1024]{1,0:T(8,128)(2,1)S(1)}, u32[]{:S(2)}, u32[]{:S(2)}) %collective-permute-start.9) | collective-permute-done | bytes 32800 | tf_op jit(solution)/shard_map/ppermute | solution.py:873
  30.6 0.0 copy-start.10
  30.6 0.0 collective-permute-done.8.refs_10_
  30.6 0.0 copy-start.11
  30.6 0.0 collective-permute-done.7.refs_8_
  30.6 0.0 copy-start.8
  30.6 0.0 collective-permute-done.5.refs_4_
  30.7 0.0 copy-start.4
  30.7 0.0 copy-done.7
  30.7 0.6 copy-done.10
  31.2 0.0 copy-done.8
  31.3 0.0 copy-done
  31.3 0.0 copy-done.1
  31.3 0.0 copy-done.3
  31.3 0.0 copy-done.9
  31.3 0.0 copy-done.11
  31.3 0.3 copy-done.4
  31.6 0.0 copy-start.2
  31.6 11.9 %final.1 = (bf16[432,1024]{1,0:T(8,128)(2,1)}, bf16[432,128]{1,0:T(8,128)(2,1)}, bf16[4,64,1024]{2,1,0:T(8,128)(2,1)}, bf16[8,16,1152]{2,1,0:T(8,128)(2,1)}) custom-call(s32[16]{0:T(128)} %owner.3, s32[16]{0:T(128)} %refs_1_.3, s32[16]{0:T(128)} %refs_2_.1, bf16[384,1024]{1,0:T(8,128)(2,1)} %copy-done.3, bf16[384,1024]{1,0:T(8,128)(2,1)} %copy-done.4, ...), custom_call_target="tpu_custom_call" | custom-call | flops 1610612736 | bytes 4194304 | tf_op jit(solution)/shard_map/final/pallas_call | solution.py:75
  43.5 5.8 %all-to-all-start.1 = ((bf16[8,16,1152]{2,1,0:T(8,128)(2,1)}), bf16[8,16,1152]{2,1,0:T(8,128)(2,1)S(1)}, u32[]{:S(2)}, u32[]{:S(2)}) async-start(bf16[8,16,1152]{2,1,0:T(8,128)(2,1)} %get-tuple-element.33), calls=%async_computation.1 | async-start | bytes 589824 | tf_op jit(solution)/shard_map/all_to_all | solution.py:906
  49.3 4.5 %outputs.1 = (bf16[384,1024]{1,0:T(8,128)(2,1)}, bf16[32,1024]{1,0:T(8,128)(2,1)}) custom-call(s32[16]{0:T(128)} %owner.3, s32[16]{0:T(128)} %refs_1_.3, bf16[432,1024]{1,0:T(8,128)(2,1)} %get-tuple-element.28.refs_2_, bf16[432,128]{1,0:T(8,128)(2,1)} %get-tuple-element.29.refs_3_, bf16[128,1024]{1,0:T(8,128)(2,1)} %refs_4_.1, f32[1,1024]{1,0:T(1,128)} %bitcast.30, ...), custom_call_target="tpu_custom_call" | custom-call | flops 805306368 | bytes 6291456 | tf_op jit(solution)/shard_map/outputs/pallas_call | solution.py:75
  53.9 4.2 %all-to-all-done.1.back = bf16[8,16,1152]{2,1,0:T(8,128)(2,1)S(1)} async-done(((bf16[8,16,1152]{2,1,0:T(8,128)(2,1)}), bf16[8,16,1152]{2,1,0:T(8,128)(2,1)S(1)}, u32[]{:S(2)}, u32[]{:S(2)}) %all-to-all-start.1) | async-done | bytes 294944 | tf_op jit(solution)/shard_map/all_to_all | solution.py:906
  58.1 0.0 copy-done.2
  58.1 1.4 %unpack.1 = (f32[16,8,1024]{2,1,0:T(8,128)}, bf16[16,8,16]{2,1,0:T(8,128)(2,1)}) custom-call(s32[16]{0:T(128)S(1)} %copy-done.2, bf16[8,16,1152]{2,1,0:T(8,128)(2,1)S(1)} %all-to-all-done.1.back), custom_call_target="tpu_custom_call" | custom-call | tf_op jit(solution)/shard_map/unpack/pallas_call | solution.py:832
Async XLA Ops:
  0.6 14.1 %collective-permute-start.2 = (bf16[384,1024]{1,0:T(8,128)(2,1)}, bf16[384,1024]{1,0:T(8,128)(2,1)S(1)}, u32[]{:S(2)}, u32[]{:S(2)}) collective-permute-start(bf16[384,1024]{1,0:T(8,128)(2,1)} %bitcast.15), channel_id=1, source_target_pairs={{0,1},{1,0},{2,3},{3,2},{4,5},{5,4},{6,7},{7,6},{8,9},{9,8},{10,11... | collective-permute-start | bytes 2359304 | tf_op jit(solution)/shard_map/ppermute | solution.py:873
  1.1 23.2 %collective-permute-start = (bf16[384,1024]{1,0:T(8,128)(2,1)}, bf16[384,1024]{1,0:T(8,128)(2,1)S(1)}, u32[]{:S(2)}, u32[]{:S(2)}) collective-permute-start(bf16[384,1024]{1,0:T(8,128)(2,1)} %bitcast.16), channel_id=1, source_target_pairs={{0,2},{1,3},{2,0},{3,1},{4,6},{5,7},{6,4},{7,5},{8,10},{9,11},{10,... | collective-permute-start | bytes 2359304 | tf_op jit(solution)/shard_map/ppermute | solution.py:873
  6.2 16.2 %all-to-all-start = ((bf16[8,16,1152]{2,1,0:T(8,128)(2,1)}), bf16[8,16,1152]{2,1,0:T(8,128)(2,1)S(1)}, u32[]{:S(2)}, u32[]{:S(2)}) async-start(bf16[8,16,1152]{2,1,0:T(8,128)(2,1)} %pack.1), calls=%async_computation | async-start | bytes 589824 | tf_op jit(solution)/shard_map/all_to_all | solution.py:882
  12.0 2.7 %collective-permute-start.3 = (f32[1,1024]{1,0:T(1,128)}, f32[1,1024]{1,0:T(1,128)S(1)}, u32[]{:S(2)}, u32[]{:S(2)}) collective-permute-start(f32[1,1024]{1,0:T(1,128)} %bitcast.23), channel_id=1, source_target_pairs={{0,1},{1,0},{2,3},{3,2},{4,5},{5,4},{6,7},{7,6},{8,9},{9,8},{10,11... | collective-permute-start | bytes 12296 | tf_op jit(solution)/shard_map/ppermute | solution.py:873
  12.0 2.7 %collective-permute-start.4 = (f32[1,1024]{1,0:T(1,128)}, f32[1,1024]{1,0:T(1,128)S(1)}, u32[]{:S(2)}, u32[]{:S(2)}) collective-permute-start(f32[1,1024]{1,0:T(1,128)} %bitcast.26), channel_id=1, source_target_pairs={{0,1},{1,0},{2,3},{3,2},{4,5},{5,4},{6,7},{7,6},{8,9},{9,8},{10,11... | collective-permute-start | bytes 12296 | tf_op jit(solution)/shard_map/ppermute | solution.py:873
  14.1 10.2 %copy-start.6 = (bf16[48,1024]{1,0:T(8,128)(2,1)S(1)}, bf16[48,1024]{1,0:T(8,128)(2,1)}, u32[]{:S(2)}) copy-start(bf16[48,1024]{1,0:T(8,128)(2,1)} %small_payload.1.refs_5_) | copy-start | bytes 294916
  14.2 10.1 %collective-permute-start.1 = (bf16[48,1024]{1,0:T(8,128)(2,1)}, bf16[48,1024]{1,0:T(8,128)(2,1)}, u32[]{:S(2)}, u32[]{:S(2)}) collective-permute-start(bf16[48,1024]{1,0:T(8,128)(2,1)} %small_payload.1.refs_5_), channel_id=1, source_target_pairs={{0,2},{1,3},{2,0},{3,1},{4,6},{5,7},{6,4},{7,5},{8,10},{9,11},{10,... | collective-permute-start | bytes 294920 | tf_op jit(solution)/shard_map/ppermute | solution.py:873
  14.7 0.6 copy-start.12
  14.7 0.6 %copy-start.13 = (f32[1,1024]{1,0:T(1,128)}, f32[1,1024]{1,0:T(1,128)S(1)}, u32[]{:S(2)}) copy-start(f32[1,1024]{1,0:T(1,128)S(1)} %collective-permute-done.4.refs_5_) | copy-start | bytes 12292
  15.3 0.9 %copy-start.5 = (bf16[384,1024]{1,0:T(8,128)(2,1)}, bf16[384,1024]{1,0:T(8,128)(2,1)S(1)}, u32[]{:S(2)}) copy-start(bf16[384,1024]{1,0:T(8,128)(2,1)S(1)} %collective-permute-done.2.refs_1_) | copy-start | bytes 2359300
  22.4 8.9 %copy-start = (bf16[8,16,1152]{2,1,0:T(8,128)(2,1)}, bf16[8,16,1152]{2,1,0:T(8,128)(2,1)S(1)}, u32[]{:S(2)}) copy-start(bf16[8,16,1152]{2,1,0:T(8,128)(2,1)S(1)} %all-to-all-done.got_in.refs_20_) | copy-start | bytes 884740
  22.7 8.6 %copy-start.1 = (bf16[16,1024]{1,0:T(8,128)(2,1)}, bf16[16,1024]{1,0:T(8,128)(2,1)S(1)}, u32[]{:S(2)}) copy-start(bf16[16,1024]{1,0:T(8,128)(2,1)S(1)} %own_inputs.1.refs_9_) | copy-start | bytes 98308
  24.3 7.0 %copy-start.3 = (bf16[384,1024]{1,0:T(8,128)(2,1)}, bf16[384,1024]{1,0:T(8,128)(2,1)S(1)}, u32[]{:S(2)}) copy-start(bf16[384,1024]{1,0:T(8,128)(2,1)S(1)} %collective-permute-done.refs_3_) | copy-start | bytes 2359300
  24.3 6.3 %collective-permute-start.5 = (bf16[384,1024]{1,0:T(8,128)(2,1)S(1)}, bf16[384,1024]{1,0:T(8,128)(2,1)S(1)}, u32[]{:S(2)}, u32[]{:S(2)}) collective-permute-start(bf16[384,1024]{1,0:T(8,128)(2,1)S(1)} %collective-permute-done.refs_3_), channel_id=1, source_target_pairs={{0,1},{1,0},{2,3},{3,2},{4,5},{5,4},{6,7},{7,6},{8,9},{9,8},{10,11... | collective-permute-start | bytes 2359304 | tf_op jit(solution)/shard_map/ppermute | solution.py:873
  24.3 2.7 %collective-permute-start.6 = (bf16[48,1024]{1,0:T(8,128)(2,1)S(1)}, bf16[48,1024]{1,0:T(8,128)(2,1)S(1)}, u32[]{:S(2)}, u32[]{:S(2)}) collective-permute-start(bf16[48,1024]{1,0:T(8,128)(2,1)S(1)} %copy-done.6), channel_id=1, source_target_pairs={{0,1},{1,0},{2,3},{3,2},{4,5},{5,4},{6,7},{7,6},{8,9},{9,8},{10,11... | collective-permute-start | bytes 294920 | tf_op jit(solution)/shard_map/ppermute | solution.py:873
  24.8 5.8 %collective-permute-start.7 = (bf16[48,1024]{1,0:T(8,128)(2,1)}, bf16[48,1024]{1,0:T(8,128)(2,1)S(1)}, u32[]{:S(2)}, u32[]{:S(2)}) collective-permute-start(bf16[48,1024]{1,0:T(8,128)(2,1)} %collective-permute-done.1.refs_7_), channel_id=1, source_target_pairs={{0,1},{1,0},{2,3},{3,2},{4,5},{5,4},{6,7},{7,6},{8,9},{9,8},{10,11... | collective-permute-start | bytes 294920 | tf_op jit(solution)/shard_map/ppermute | solution.py:873
  24.9 3.4 %collective-permute-start.10 = (bf16[16,1024]{1,0:T(8,128)(2,1)S(1)}, bf16[16,1024]{1,0:T(8,128)(2,1)S(1)}, u32[]{:S(2)}, u32[]{:S(2)}) collective-permute-start(bf16[16,1024]{1,0:T(8,128)(2,1)S(1)} %own_inputs.1.refs_9_), channel_id=1, source_target_pairs={{0,3},{1,2},{2,1},{3,0},{4,7},{5,6},{6,5},{7,4},{8,11},{9,10},{10,... | collective-permute-start | bytes 98312 | tf_op jit(solution)/shard_map/ppermute | solution.py:873
  26.7 3.9 %collective-permute-start.9 = (bf16[16,1024]{1,0:T(8,128)(2,1)S(1)}, bf16[16,1024]{1,0:T(8,128)(2,1)S(1)}, u32[]{:S(2)}, u32[]{:S(2)}) collective-permute-start(bf16[16,1024]{1,0:T(8,128)(2,1)S(1)} %own_inputs.1.refs_9_), channel_id=1, source_target_pairs={{0,2},{1,3},{2,0},{3,1},{4,6},{5,7},{6,4},{7,5},{8,10},{9,11},{10,... | collective-permute-start | bytes 98312 | tf_op jit(solution)/shard_map/ppermute | solution.py:873
  27.0 3.7 %copy-start.7 = (bf16[48,1024]{1,0:T(8,128)(2,1)}, bf16[48,1024]{1,0:T(8,128)(2,1)S(1)}, u32[]{:S(2)}) copy-start(bf16[48,1024]{1,0:T(8,128)(2,1)S(1)} %collective-permute-done.6.refs_6_) | copy-start | bytes 294916
  27.0 3.6 %collective-permute-start.8 = (bf16[16,1024]{1,0:T(8,128)(2,1)S(1)}, bf16[16,1024]{1,0:T(8,128)(2,1)S(1)}, u32[]{:S(2)}, u32[]{:S(2)}) collective-permute-start(bf16[16,1024]{1,0:T(8,128)(2,1)S(1)} %own_inputs.1.refs_9_), channel_id=1, source_target_pairs={{0,1},{1,0},{2,3},{3,2},{4,5},{5,4},{6,7},{7,6},{8,9},{9,8},{10,11... | collective-permute-start | bytes 98312 | tf_op jit(solution)/shard_map/ppermute | solution.py:873
  28.3 3.0 %copy-start.9 = (bf16[16,1024]{1,0:T(8,128)(2,1)}, bf16[16,1024]{1,0:T(8,128)(2,1)S(1)}, u32[]{:S(2)}) copy-start(bf16[16,1024]{1,0:T(8,128)(2,1)S(1)} %collective-permute-done.10.refs_12_) | copy-start | bytes 98308
  30.6 0.6 %copy-start.10 = (bf16[16,1024]{1,0:T(8,128)(2,1)}, bf16[16,1024]{1,0:T(8,128)(2,1)S(1)}, u32[]{:S(2)}) copy-start(bf16[16,1024]{1,0:T(8,128)(2,1)S(1)} %collective-permute-done.9.refs_11_) | copy-start | bytes 98308
  30.6 0.7 %copy-start.11 = (bf16[16,1024]{1,0:T(8,128)(2,1)}, bf16[16,1024]{1,0:T(8,128)(2,1)S(1)}, u32[]{:S(2)}) copy-start(bf16[16,1024]{1,0:T(8,128)(2,1)S(1)} %collective-permute-done.8.refs_10_) | copy-start | bytes 98308
  30.6 0.6 %copy-start.8 = (bf16[48,1024]{1,0:T(8,128)(2,1)}, bf16[48,1024]{1,0:T(8,128)(2,1)S(1)}, u32[]{:S(2)}) copy-start(bf16[48,1024]{1,0:T(8,128)(2,1)S(1)} %collective-permute-done.7.refs_8_) | copy-start | bytes 294916
  30.7 0.9 %copy-start.4 = (bf16[384,1024]{1,0:T(8,128)(2,1)}, bf16[384,1024]{1,0:T(8,128)(2,1)S(1)}, u32[]{:S(2)}) copy-start(bf16[384,1024]{1,0:T(8,128)(2,1)S(1)} %collective-permute-done.5.refs_4_) | copy-start | bytes 2359300
  31.6 26.5 %copy-start.2 = (s32[16]{0:T(128)S(1)}, s32[16]{0:T(128)}, u32[]{:S(2)}) copy-start(s32[16]{0:T(128)} %owner.3) | copy-start | bytes 196
  43.5 14.6 %all-to-all-start.1 = ((bf16[8,16,1152]{2,1,0:T(8,128)(2,1)}), bf16[8,16,1152]{2,1,0:T(8,128)(2,1)S(1)}, u32[]{:S(2)}, u32[]{:S(2)}) async-start(bf16[8,16,1152]{2,1,0:T(8,128)(2,1)} %get-tuple-element.33), calls=%async_computation.1 | async-start | bytes 589824 | tf_op jit(solution)/shard_map/all_to_all | solution.py:906
